TPU v7x, 32 devices: a whole 2x2x4 slice. The times are simulated.
32 devices in a mesh: wide: 8 (over z, y), narrow: 4 (over x, core).
Axes of the slice: x: 2, y: 2, z: 4, core: 2. Of those that a mesh axis runs over, the one named last changes fastest.
Arguments:
- tokens: bfloat16 [34816, 768], P(('wide', 'narrow')), may hold values from -6 to 6
- cotangent: bfloat16 [34816, 768], P(('wide', 'narrow')), may hold values from -6 to 6
- latents: bfloat16 [34816, 16], P(('wide', 'narrow')), may hold values from -6 to 6
- added_noise: float32 [4, 16, 8192], P(None, None, ('wide', 'narrow')), may hold values from -6 to 6
- timesteps: int32 [4, 8192], P(None, ('wide', 'narrow')), may hold values from 0 to 999
- bucket: int32 [32], replicated, may hold values from 256 to 1024, as said below
- masked: int32 [32, 1088], P(('wide', 'narrow')), may hold values from 0 to 1, as said below
- deal_start: int32 [32], replicated, may hold values from 0 to 7
- first_gain: float32 [768], replicated, may hold values from 0.5 to 1.5
- first_shift: float32 [768], replicated, may hold values from -0.3125 to 0.3125
- joint_weight: bfloat16 [768, 2304], replicated, may hold values from -0.21875 to 0.21875
- query_value_bias: float32 [1536], replicated, may hold values from -0.3125 to 0.3125
- output_weight: bfloat16 [768, 768], replicated, may hold values from -1.5 to 1.5
- output_bias: float32 [768], replicated, may hold values from -0.3125 to 0.3125
- second_gain: float32 [768], replicated, may hold values from 0.5 to 1.5
- second_shift: float32 [768], replicated, may hold values from -0.3125 to 0.3125
- expand_weight: bfloat16 [768, 3072], replicated, may hold values from -0.21875 to 0.21875
- expand_bias: float32 [3072], replicated, may hold values from -1.25 to 1.25
- reduce_weight: bfloat16 [3072, 768], replicated, may hold values from -0.109375 to 0.109375
- reduce_bias: float32 [768], replicated, may hold values from -0.3125 to 0.3125
- input_proj: bfloat16 [1024, 16], replicated, may hold values from -1.5 to 1.5
- cond_proj: bfloat16 [768, 1024], replicated, may hold values from -0.21875 to 0.21875
- time_first: bfloat16 [256, 1024], replicated, may hold values from -0.375 to 0.375
- time_second: bfloat16 [1024, 1024], replicated, may hold values from -0.1875 to 0.1875
- block_mod: bfloat16 [1024, 3072], replicated, may hold values from -0.1875 to 0.1875
- block_expand: bfloat16 [1024, 1024], replicated, may hold values from -0.1875 to 0.1875
- block_reduce: bfloat16 [1024, 1024], replicated, may hold values from -0.1875 to 0.1875
- final_mod: bfloat16 [1024, 2048], replicated, may hold values from -0.1875 to 0.1875
- final_proj: bfloat16 [1024, 16], replicated, may hold values from -0.375 to 0.375
Outputs:
- block_output: bfloat16 [34816, 768], P(('wide', 'narrow'))
- noise_guess: float32 [4, 16, 8192], P(None, None, ('wide', 'narrow'))
- branch_spread: float32 [32, 2], P(('wide', 'narrow'))
- tokens_gradient: float32 [34816, 768], P(('wide', 'narrow'))
- first_gain_gradient: float32 [768], P('wide')
- first_shift_gradient: float32 [768], P('wide')
- joint_weight_gradient: float32 [768, 2304], P('wide')
- query_value_bias_gradient: float32 [1536], P('wide')
- output_weight_gradient: float32 [768, 768], P('wide')
- output_bias_gradient: float32 [768], P('wide')
- second_gain_gradient: float32 [768], P('wide')
- second_shift_gradient: float32 [768], P('wide')
- expand_weight_gradient: float32 [768, 3072], P('wide')
- expand_bias_gradient: float32 [3072], P('wide')
- reduce_weight_gradient: float32 [3072, 768], P('wide')
- reduce_bias_gradient: float32 [768], P('wide')
- input_proj_gradient: float32 [1024, 16], P('wide')
- cond_proj_gradient: float32 [768, 1024], P('wide')
- time_first_gradient: float32 [256, 1024], P('wide')
- time_second_gradient: float32 [1024, 1024], P('wide')
- block_mod_gradient: float32 [1024, 3072], P('wide')
- block_expand_gradient: float32 [1024, 1024], P('wide')
- block_reduce_gradient: float32 [1024, 1024], P('wide')
- final_mod_gradient: float32 [1024, 2048], P('wide')
- final_proj_gradient: float32 [1024, 16], P('wide')
Inputs may be any that keep to these rules, and one draw needn't show every extreme that they name: `bucket`: each entry is 256 or 1024; among the images whose index has one remainder modulo 4, at least one has 1024. `masked`: row i has exactly bucket[i] * 256 // 1024 ones, all at positions 64 to 64 + bucket[i] - 1.
All inputs are finite; a program needn't handle non-finite values.
Results may differ from a plain program's by a relative error of at most 0.017.
Values may be sent and summed in bfloat16 or wider, within the bound.
No kernel may reach another device: no remote copies, remote signals or barrier semaphores. Data moves between devices by JAX's collectives and lax.ppermute only.
A program may use at most 320 MiB of HBM per device.

v0:
```python
from functools import partial
import math

import jax
import jax.numpy as jnp
from jax import lax
from jax.sharding import PartitionSpec as P

D = 768
HEADS = 12
HEAD_DIM = 64
TOKEN_DIM = 16
BUFFER = 64
IMAGE_MAX = 1024
MASK_MAX = 256
REPEATS = 4
SEQ = 1088


SHIFT_ANGLE = 0.008 / 1.008 * math.pi / 2.0
STEP_ANGLE = math.pi / (2.0 * 1.008 * 1000.0)


def for_sending(shard):
    return jax.tree.map(lambda a: a.astype(jnp.bfloat16) if a.dtype == jnp.float32 else a, shard)


def matmul(left, right):
    return jnp.dot(left, right, preferred_element_type=jnp.float32)


def contract_rows(left, right):
    return lax.dot_general(
        left, right, (((0,), (0,)), ((), ())), preferred_element_type=jnp.float32
    )


def contract_last(left, right):
    return lax.dot_general(
        left, right, (((1,), (1,)), ((), ())), preferred_element_type=jnp.float32
    )


def normalize(values):
    centre = values - jnp.mean(values, axis=-1, keepdims=True)
    inverse = lax.rsqrt(jnp.mean(centre * centre, axis=-1, keepdims=True) + 1e-06)
    return (centre * inverse, inverse)


def normalize_back(grad_normed, normed, inverse):
    return inverse * (
        grad_normed
        - jnp.mean(grad_normed, axis=-1, keepdims=True)
        - normed * jnp.mean(grad_normed * normed, axis=-1, keepdims=True)
    )


def silu_back(before, grad_after):
    sigma = jax.nn.sigmoid(before)
    return grad_after * sigma * (1.0 + before * (1.0 - sigma))


def to_heads(array):
    return array.reshape(array.shape[0], HEADS, HEAD_DIM).transpose(1, 0, 2)


def from_heads(array):
    return array.transpose(1, 0, 2).reshape(array.shape[1], HEADS * HEAD_DIM)


def attend(query, keys, values, keep_keys, scale):

    def single(inputs):
        head_query, head_keys, head_values = inputs
        scores = jnp.where(keep_keys[None, :], contract_last(head_query, head_keys) * scale, -1e30)
        top = jnp.max(scores, axis=-1, keepdims=True)
        total = jnp.sum(jnp.exp(scores - top), axis=-1, keepdims=True)
        logsum = top + jnp.log(total)
        probs = jnp.exp(scores - logsum).astype(jnp.bfloat16)
        return (matmul(probs, head_values).astype(jnp.bfloat16), logsum[:, 0])

    return lax.map(single, (query, keys, values))


def attend_back(query, keys, values, logsum, grad_mixed, keep_keys, scale):

    def single(inputs):
        head_query, head_keys, head_values, head_logsum, head_grad = inputs
        scores = jnp.where(keep_keys[None, :], contract_last(head_query, head_keys) * scale, -1e30)
        probs = jnp.exp(scores - head_logsum[:, None])
        grad_probs = contract_last(head_grad, head_values)
        across = jnp.sum(probs * grad_probs, axis=-1, keepdims=True)
        grad_scores = (probs * (grad_probs - across)).astype(jnp.bfloat16)
        grad_query = (matmul(grad_scores, head_keys) * scale).astype(jnp.bfloat16)
        grad_keys = (contract_rows(grad_scores, head_query) * scale).astype(jnp.bfloat16)
        grad_values = contract_rows(probs.astype(jnp.bfloat16), head_grad).astype(jnp.bfloat16)
        return (grad_query, grad_keys, grad_values)

    return lax.map(single, (query, keys, values, logsum, grad_mixed))


def diffusion_pass(rows, latent, noise_part, steps, live, weights):
    (
        input_proj,
        cond_proj,
        time_first,
        time_second,
        block_mod,
        block_expand,
        block_reduce,
        final_mod,
        final_proj,
    ) = weights
    width = cond_proj.shape[1]
    embed = matmul(rows, cond_proj)
    half = time_first.shape[0] // 2
    freqs = jnp.exp(-math.log(10000.0) * jnp.arange(half).astype(jnp.float32) / half)
    angles = steps[:, :, None] * freqs
    sinus = jnp.concatenate([jnp.cos(angles), jnp.sin(angles)], axis=-1).astype(jnp.bfloat16)
    first = jnp.einsum("rsf,fw->rsw", sinus, time_first, preferred_element_type=jnp.float32)
    first_low = jax.nn.silu(first).astype(jnp.bfloat16)
    timed = jnp.einsum("rsw,wv->rsv", first_low, time_second, preferred_element_type=jnp.float32)
    cond_all = embed[None] + timed
    acted = jax.nn.silu(cond_all).astype(jnp.bfloat16)
    modul = jnp.einsum("rsw,wv->rsv", acted, block_mod, preferred_element_type=jnp.float32)
    finmod = jnp.einsum("rsw,wv->rsv", acted, final_mod, preferred_element_type=jnp.float32)
    shift_a = modul[..., :width]
    scale_a = modul[..., width : 2 * width]
    gate_a = modul[..., 2 * width :]
    shift_b = finmod[..., :width]
    scale_b = finmod[..., width:]
    offset = steps * STEP_ANGLE
    keep_sig = jnp.cos(offset + SHIFT_ANGLE) / math.cos(SHIFT_ANGLE)
    drop_sig = jnp.sqrt(jnp.sin(offset) * jnp.sin(offset + 2.0 * SHIFT_ANGLE)) / math.cos(
        SHIFT_ANGLE
    )
    noisy = (
        keep_sig[:, None, :] * latent.astype(jnp.float32).T[None]
        + drop_sig[:, None, :] * noise_part
    ).astype(jnp.bfloat16)
    entry = jnp.einsum("rcs,wc->rsw", noisy, input_proj, preferred_element_type=jnp.float32)
    inner_normed, inner_inverse = normalize(entry)
    inner = (inner_normed * (1.0 + scale_a) + shift_a).astype(jnp.bfloat16)
    upper = jnp.einsum("rsw,wv->rsv", inner, block_expand, preferred_element_type=jnp.float32)
    lifted = jax.nn.silu(upper).astype(jnp.bfloat16)
    branch = jnp.einsum("rsw,wv->rsv", lifted, block_reduce, preferred_element_type=jnp.float32)
    after = entry + gate_a * branch
    last_normed, last_inverse = normalize(after)
    last = (last_normed * (1.0 + scale_b) + shift_b).astype(jnp.bfloat16)
    masking = live[None, None, :]
    guess = (
        jnp.einsum("rsw,wc->rcs", last, final_proj, preferred_element_type=jnp.float32) * masking
    )
    miss = guess - noise_part * masking
    grad_guess = (2.0 / REPEATS * miss * masking).astype(jnp.bfloat16)
    final_proj_grad = jnp.einsum(
        "rsw,rcs->wc", last, grad_guess, preferred_element_type=jnp.float32
    )
    grad_last = jnp.einsum(
        "rcs,wc->rsw", grad_guess, final_proj, preferred_element_type=jnp.float32
    )
    grad_scale_b = grad_last * last_normed
    grad_after = normalize_back(grad_last * (1.0 + scale_b), last_normed, last_inverse)
    grad_gate = grad_after * branch
    grad_branch = (grad_after * gate_a).astype(jnp.bfloat16)
    block_reduce_grad = jnp.einsum(
        "rsw,rsv->wv", lifted, grad_branch, preferred_element_type=jnp.float32
    )
    grad_lifted = jnp.einsum(
        "rsv,wv->rsw", grad_branch, block_reduce, preferred_element_type=jnp.float32
    )
    grad_upper = silu_back(upper, grad_lifted).astype(jnp.bfloat16)
    block_expand_grad = jnp.einsum(
        "rsw,rsv->wv", inner, grad_upper, preferred_element_type=jnp.float32
    )
    grad_inner = jnp.einsum(
        "rsv,wv->rsw", grad_upper, block_expand, preferred_element_type=jnp.float32
    )
    grad_scale_a = grad_inner * inner_normed
    grad_entry = (
        grad_after + normalize_back(grad_inner * (1.0 + scale_a), inner_normed, inner_inverse)
    ).astype(jnp.bfloat16)
    input_proj_grad = jnp.einsum(
        "rsw,rcs->wc", grad_entry, noisy, preferred_element_type=jnp.float32
    )
    grad_modul = jnp.concatenate([grad_inner, grad_scale_a, grad_gate], axis=-1).astype(
        jnp.bfloat16
    )
    grad_finmod = jnp.concatenate([grad_last, grad_scale_b], axis=-1).astype(jnp.bfloat16)
    block_mod_grad = jnp.einsum(
        "rsw,rsv->wv", acted, grad_modul, preferred_element_type=jnp.float32
    )
    final_mod_grad = jnp.einsum(
        "rsw,rsv->wv", acted, grad_finmod, preferred_element_type=jnp.float32
    )
    grad_acted = jnp.einsum(
        "rsv,wv->rsw", grad_modul, block_mod, preferred_element_type=jnp.float32
    ) + jnp.einsum("rsv,wv->rsw", grad_finmod, final_mod, preferred_element_type=jnp.float32)
    grad_cond = silu_back(cond_all, grad_acted)
    grad_timed = grad_cond.astype(jnp.bfloat16)
    time_second_grad = jnp.einsum(
        "rsw,rsv->wv", first_low, grad_timed, preferred_element_type=jnp.float32
    )
    grad_first = silu_back(
        first,
        jnp.einsum("rsv,wv->rsw", grad_timed, time_second, preferred_element_type=jnp.float32),
    ).astype(jnp.bfloat16)
    time_first_grad = jnp.einsum(
        "rsf,rsw->fw", sinus, grad_first, preferred_element_type=jnp.float32
    )
    grad_embed = jnp.sum(grad_cond, axis=0).astype(jnp.bfloat16)
    cond_proj_grad = contract_rows(rows, grad_embed)
    grad_rows = contract_last(grad_embed, cond_proj)
    return (
        guess,
        grad_rows,
        (
            input_proj_grad,
            cond_proj_grad,
            time_first_grad,
            time_second_grad,
            block_mod_grad,
            block_expand_grad,
            block_reduce_grad,
            final_mod_grad,
            final_proj_grad,
        ),
    )


def shards(
    tokens,
    cotangent,
    latents,
    added_noise,
    timesteps,
    bucket,
    masked,
    deal_start,
    first_gain,
    first_shift,
    joint_weight,
    query_value_bias,
    output_weight,
    output_bias,
    second_gain,
    second_shift,
    expand_weight,
    expand_bias,
    reduce_weight,
    reduce_bias,
    input_proj,
    cond_proj,
    time_first,
    time_second,
    block_mod,
    block_expand,
    block_reduce,
    final_mod,
    final_proj,
):
    wide_count = lax.axis_size("wide")
    narrow_count = lax.axis_size("narrow")
    capacity = MASK_MAX // wide_count
    place_wide = lax.axis_index("wide")
    place_narrow = lax.axis_index("narrow")
    image_index = place_wide * narrow_count + place_narrow
    length = BUFFER + bucket[image_index]
    keep_keys = jnp.arange(SEQ) < length
    keep_rows = keep_keys.astype(jnp.float32)[:, None]
    scale = HEAD_DIM ** (-0.5)
    image = tokens.astype(jnp.float32)
    first_normed, first_inverse = normalize(image)
    first_in = (first_normed * first_gain + first_shift).astype(jnp.bfloat16)
    joint = matmul(first_in, joint_weight)
    query = to_heads((joint[:, :D] + query_value_bias[:D]).astype(jnp.bfloat16))
    keys = to_heads(joint[:, D : 2 * D].astype(jnp.bfloat16))
    values = to_heads((joint[:, 2 * D :] + query_value_bias[D:]).astype(jnp.bfloat16))
    mixed_heads, logsum = attend(query, keys, values, keep_keys, scale)
    mixed = from_heads(mixed_heads)
    branch = matmul(mixed, output_weight) + output_bias
    middle = image + branch
    second_normed, second_inverse = normalize(middle)
    second_in = (second_normed * second_gain + second_shift).astype(jnp.bfloat16)
    hidden = matmul(second_in, expand_weight) + expand_bias
    active, gelu_back = jax.vjp(partial(jax.nn.gelu, approximate=False), hidden)
    active_low = active.astype(jnp.bfloat16)
    feed = matmul(active_low, reduce_weight) + reduce_bias
    result = (middle + feed) * keep_rows
    block_output = result.astype(jnp.bfloat16)
    count = length.astype(jnp.float32) * D
    spread = jnp.stack(
        [
            jnp.sqrt(jnp.sum(keep_rows * branch * branch) / count),
            jnp.sqrt(jnp.sum(keep_rows * feed * feed) / count),
        ]
    )[None, :]
    chosen = masked[0] > 0
    order = jnp.cumsum(masked[0]) - 1
    target = jnp.where(
        chosen,
        (deal_start[image_index] + order) % wide_count * capacity + order // wide_count,
        wide_count * capacity,
    )
    send_rows = (
        jnp.zeros((wide_count * capacity + 1, D), jnp.bfloat16).at[target].set(block_output)[:-1]
    )
    send_latent = (
        jnp.zeros((wide_count * capacity + 1, TOKEN_DIM), jnp.bfloat16).at[target].set(latents)[:-1]
    )
    head_weights = (
        input_proj,
        cond_proj,
        time_first,
        time_second,
        block_mod,
        block_expand,
        block_reduce,
        final_mod,
        final_proj,
    )
    got_rows, got_latent = (
        lax.all_to_all(
            send_rows.reshape(wide_count, capacity, D),
            "wide",
            split_axis=0,
            concat_axis=0,
            tiled=True,
        ),
        lax.all_to_all(
            send_latent.reshape(wide_count, capacity, TOKEN_DIM),
            "wide",
            split_axis=0,
            concat_axis=0,
            tiled=True,
        ),
    )
    sources = jnp.arange(wide_count) * narrow_count + place_narrow
    source_count = bucket[sources] * MASK_MAX // IMAGE_MAX
    first_rank = (place_wide - deal_start[sources]) % wide_count
    arrived = jnp.maximum((source_count - first_rank + wide_count - 1) // wide_count, 0)
    live = (jnp.arange(capacity)[None, :] < arrived[:, None]).astype(jnp.float32).reshape(-1)
    guess, grad_rows, head_grads = diffusion_pass(
        got_rows.reshape(-1, D),
        got_latent.reshape(-1, TOKEN_DIM),
        added_noise,
        timesteps.astype(jnp.float32),
        live,
        head_weights,
    )
    returned = lax.all_to_all(
        grad_rows.astype(jnp.bfloat16).reshape(wide_count, capacity, D),
        "wide",
        split_axis=0,
        concat_axis=0,
        tiled=True,
    ).reshape(-1, D)
    padded = jnp.concatenate([returned, jnp.zeros((1, D), jnp.bfloat16)], axis=0)
    head_to_tokens = padded[target].astype(jnp.float32)
    grad_out = (cotangent.astype(jnp.float32) + head_to_tokens) * keep_rows
    grad_feed = grad_out.astype(jnp.bfloat16)
    reduce_weight_grad = contract_rows(active_low, grad_feed)
    reduce_bias_grad = jnp.sum(grad_feed.astype(jnp.float32), axis=0)
    grad_active = contract_last(grad_feed, reduce_weight)
    grad_hidden = gelu_back(grad_active)[0].astype(jnp.bfloat16)
    expand_weight_grad = contract_rows(second_in, grad_hidden)
    expand_bias_grad = jnp.sum(grad_hidden.astype(jnp.float32), axis=0)
    grad_second = contract_last(grad_hidden, expand_weight)
    second_gain_grad = jnp.sum(grad_second * second_normed, axis=0)
    second_shift_grad = jnp.sum(grad_second, axis=0)
    grad_middle = grad_out + normalize_back(
        grad_second * second_gain, second_normed, second_inverse
    )
    grad_branch = grad_middle.astype(jnp.bfloat16)
    output_weight_grad = contract_rows(mixed, grad_branch)
    output_bias_grad = jnp.sum(grad_branch.astype(jnp.float32), axis=0)
    grad_mixed = to_heads(contract_last(grad_branch, output_weight).astype(jnp.bfloat16))
    grad_query, grad_keys, grad_values = attend_back(
        query, keys, values, logsum, grad_mixed, keep_keys, scale
    )
    grad_query = from_heads(grad_query)
    grad_values = from_heads(grad_values)
    grad_joint = jnp.concatenate([grad_query, from_heads(grad_keys), grad_values], axis=1)
    joint_weight_grad = contract_rows(first_in, grad_joint)
    query_value_bias_grad = jnp.concatenate(
        [
            jnp.sum(grad_query.astype(jnp.float32), axis=0),
            jnp.sum(grad_values.astype(jnp.float32), axis=0),
        ]
    )
    grad_first = contract_last(grad_joint, joint_weight)
    first_gain_grad = jnp.sum(grad_first * first_normed, axis=0)
    first_shift_grad = jnp.sum(grad_first, axis=0)
    tokens_gradient = grad_middle + normalize_back(
        grad_first * first_gain, first_normed, first_inverse
    )
    local_grads = (
        first_gain_grad,
        first_shift_grad,
        joint_weight_grad,
        query_value_bias_grad,
        output_weight_grad,
        output_bias_grad,
        second_gain_grad,
        second_shift_grad,
        expand_weight_grad,
        expand_bias_grad,
        reduce_weight_grad,
        reduce_bias_grad,
    ) + tuple(head_grads)
    shares = jax.tree.map(
        lambda part: part.astype(jnp.float32),
        lax.psum_scatter(for_sending(local_grads), "wide", scatter_dimension=0, tiled=True),
    )
    totals = jax.tree.map(
        lambda part: part.astype(jnp.float32), lax.psum(for_sending(shares), "narrow")
    )
    return (block_output, guess, spread, tokens_gradient) + tuple(totals)


def solution(mesh):
    in_specs = (
        P(("wide", "narrow"), None),
        P(("wide", "narrow"), None),
        P(("wide", "narrow"), None),
        P(None, None, ("wide", "narrow")),
        P(None, ("wide", "narrow")),
        P(),
        P(("wide", "narrow"), None),
        P(),
        P(),
        P(),
        P(),
        P(),
        P(),
        P(),
        P(),
        P(),
        P(),
        P(),
        P(),
        P(),
        P(),
        P(),
        P(),
        P(),
        P(),
        P(),
        P(),
        P(),
        P(),
    )
    out_specs = (
        P(("wide", "narrow"), None),
        P(None, None, ("wide", "narrow")),
        P(("wide", "narrow"), None),
        P(("wide", "narrow"), None),
        P("wide"),
        P("wide"),
        P("wide", None),
        P("wide"),
        P("wide", None),
        P("wide"),
        P("wide"),
        P("wide"),
        P("wide", None),
        P("wide"),
        P("wide", None),
        P("wide"),
        P("wide", None),
        P("wide", None),
        P("wide", None),
        P("wide", None),
        P("wide", None),
        P("wide", None),
        P("wide", None),
        P("wide", None),
        P("wide", None),
    )
    return jax.shard_map(shards, mesh=mesh, in_specs=in_specs, out_specs=out_specs, check_vma=False)
```

profile of v0, /device:TPU:0, one launch (start us, length us, event | category | flops | bytes accessed | tf_op | source)
XLA Modules:
  0.0 1515.4 jit_solution(13205532331479377586)
XLA Ops:
  87.8 79.3 %while.28 = (s32[]{:T(128)}, bf16[12,1088,64]{1,2,0:T(8,128)(2,1)}, f32[12,1088]{1,0:T(8,128)}, bf16[12,1088,64]{2,1,0:T(8,128)(2,1)}, bf16[12,1088,64]{2,1,0:T(...) while((s32[]{:T(128)}, bf16[12,1088,64]{1,2,0:T(8,128)(2,1)}, ...), condition=%wide.region_5.6_spmd.clone, body=%wide.region_2.5_spmd.clone.sunk | while | flops 311394304 | bytes 15240173 | solution.py:82
  177.9 36.7 %multiply_convert_fusion.1 = (bf16[1088,3072]{1,0:T(8,128)(2,1)S(1)}, f32[1088,3072]{1,0:T(8,128)}, f32[1088,3072]{1,0:T(8,128)}) fusion(f32[3072]{0:T(1024)S(1)} %copy-done.61, bf16[768,3072]{1,0:T(8,128)(2,1)S(1)} %bitcast.278, f32[1088,768]{1,0:T(8,128)S(1)} %get-tuple-element.301, f32[768]{0:T(1024)S(1)} %copy-done.63, f32[768]{0:T(1024)S(1)} %copy-done.56, ...), kind=kOutput, calls=%fused_computation.71 | convolution fusion | flops 5358600192 | bytes 41511424 | tf_op jit(solution)/shard_map/dot_general | solution.py:29
  225.4 9.9 scatter_custom_fusion.1
  312.1 9.5 multiply_convert_fusion.6
  341.5 15.1 fusion.173
  400.8 19.5 %fusion.174 = (bf16[3072]{0:T(1024)(128)(2,1)}, bf16[1088,3072]{1,0:T(8,128)(2,1)}) fusion(f32[1088,3072]{1,0:T(8,128)} %get-tuple-element.299, f32[1088,3072]{1,0:T(8,128)} %get-tuple-element.320, bf16[1088,768]{1,0:T(8,128)(2,1)} %get-tuple-element.291, bf16[3072,768]{1,0:T(8,128)(2,1)} %param.51), kind=kOutput, calls=%fused_computation.307 | convolution fusion | flops 5183960064 | bytes 39819264 | tf_op jit(solution)/shard_map/dot_general | solution.py:39
  420.4 12.2 multiply_reduce_fusion.5
  475.6 158.0 %while.29 = (s32[]{:T(128)}, bf16[12,1088,64]{1,2,0:T(8,128)(2,1)}, bf16[12,1088,64]{1,2,0:T(8,128)(2,1)}, bf16[12,1088,64]{1,2,0:T(8,128)(2,1)}, bf16[12,1088,6...) while((s32[]{:T(128)}, bf16[12,1088,64]{1,2,0:T(8,128)(2,1)}, ...), condition=%wide.region_25.26_spmd.clone, body=%wide.region_23.25_spmd.clone.sunk | while | flops 768598016 | bytes 37671420 | solution.py:99
  633.6 10.3 convolution_convert_fusion.2
  644.1 9.5 bitcast_convert_fusion.1
  653.7 11.9 convolution_convert_fusion.1
  665.6 10.5 convolution_convert_fusion
  676.4 12.9 bitcast_convert_fusion
  697.7 67.1 %reduce-scatter.30.cloned.1.call-done = bf16[128,1024]{1,0:T(8,128)(2,1)} async-done(((bf16[1024,1024]{1,0:T(8,128)(2,1)}), bf16[128,1024]{1,0:T(8,128)(2,1)}) %reduce-scatter.30.cloned.1.call-update) | async-done | bytes 262160 | tf_op jit(solution)/shard_map/reduce_scatter | solution.py:413
  764.8 70.3 %reduce-scatter.34.cloned.1.call-done = bf16[128,1024]{1,0:T(8,128)(2,1)} async-done(((bf16[1024,1024]{1,0:T(8,128)(2,1)}), bf16[128,1024]{1,0:T(8,128)(2,1)}) %reduce-scatter.34.cloned.1.call-update) | async-done | bytes 262160 | tf_op jit(solution)/shard_map/reduce_scatter | solution.py:413
  835.1 70.1 %reduce-scatter.36.cloned.1.call-done = bf16[128,1024]{1,0:T(8,128)(2,1)} async-done(((bf16[1024,1024]{1,0:T(8,128)(2,1)}), bf16[128,1024]{1,0:T(8,128)(2,1)}) %reduce-scatter.36.cloned.1.call-update) | async-done | bytes 262160 | tf_op jit(solution)/shard_map/reduce_scatter | solution.py:413
  905.2 81.8 %reduce-scatter.18.cloned.1.call-done = bf16[96,2304]{1,0:T(8,128)(2,1)} async-done(((bf16[768,2304]{1,0:T(8,128)(2,1)}), bf16[96,2304]{1,0:T(8,128)(2,1)}) %reduce-scatter.18.cloned.1.call-update) | async-done | bytes 442384 | tf_op jit(solution)/shard_map/reduce_scatter | solution.py:413
  987.0 91.0 %reduce-scatter.38.cloned.1.call-done = bf16[128,2048]{1,0:T(8,128)(2,1)} async-done(((bf16[1024,2048]{1,0:T(8,128)(2,1)}), bf16[128,2048]{1,0:T(8,128)(2,1)}) %reduce-scatter.38.cloned.1.call-update) | async-done | bytes 524304 | tf_op jit(solution)/shard_map/reduce_scatter | solution.py:413
  1078.0 99.3 %reduce-scatter.22.cloned.1.call-done = bf16[96,3072]{1,0:T(8,128)(2,1)} async-done(((bf16[768,3072]{1,0:T(8,128)(2,1)}), bf16[96,3072]{1,0:T(8,128)(2,1)}) %reduce-scatter.22.cloned.1.call-update) | async-done | bytes 589840 | tf_op jit(solution)/shard_map/reduce_scatter | solution.py:413
  1177.3 99.1 %reduce-scatter.24.cloned.1.call-done = bf16[384,768]{1,0:T(8,128)(2,1)} async-done(((bf16[3072,768]{1,0:T(8,128)(2,1)}), bf16[384,768]{1,0:T(8,128)(2,1)}) %reduce-scatter.24.cloned.1.call-update) | async-done | bytes 589840 | tf_op jit(solution)/shard_map/reduce_scatter | solution.py:413
  1276.4 121.8 %reduce-scatter.32.cloned.1.call-done = bf16[128,3072]{1,0:T(8,128)(2,1)} async-done(((bf16[1024,3072]{1,0:T(8,128)(2,1)}), bf16[128,3072]{1,0:T(8,128)(2,1)}) %reduce-scatter.32.cloned.1.call-update) | async-done | bytes 786448 | tf_op jit(solution)/shard_map/reduce_scatter | solution.py:413
  1398.2 10.7 fusion.88
  1416.2 36.6 %all-reduce.10 = (bf16[768]{0:T(1024)(128)(2,1)}, bf16[768]{0:T(1024)(128)(2,1)}, bf16[1536]{0:T(1024)(128)(2,1)}, bf16[768]{0:T(1024)(128)(2,1)}, bf16[768]{0:T...) all-reduce(bf16[768]{0:T(1024)(128)(2,1)} %get-tuple-element.219, ...), channel_id=2, replica_groups=mesh['wide'=8,'narrow'=4] {'wide'}, use_global_device_ids=true, to_apply=%region_29.30.clone | all-reduce | flops 9216 | bytes 36864
  1463.0 12.4 all-reduce.11
  (510 shorter events, 577.6 us)
Async XLA Ops:
  7.2 43.9 %copy-start = (bf16[768,2304]{1,0:T(8,128)(2,1)S(1)}, bf16[768,2304]{1,0:T(8,128)(2,1)}, u32[]{:S(2)}) copy-start(bf16[768,2304]{1,0:T(8,128)(2,1)} %param.43) | copy-start | bytes 10616836
  28.8 208.3 %all-to-all-start = ((bf16[8,2,256]{2,1,0:T(2,128)(2,1)}), bf16[8,2,256]{2,1,0:T(2,128)(2,1)}, u32[]{:S(2)}, u32[]{:S(2)}) async-start(bf16[8,2,256]{2,1,0:T(2,128)(2,1)} %reshape.432), calls=%async_computation | async-start | bytes 16384 | tf_op jit(solution)/shard_map/all_to_all | solution.py:330
  86.4 128.2 %copy-start.37 = (f32[1088]{0:T(1024)}, f32[1088]{0:T(1024)S(1)}, u32[]{:S(2)}) copy-start(f32[1088]{0:T(1024)S(1)} %fusion.139) | copy-start | bytes 13060
  171.5 43.1 %copy-start.8 = (f32[1088,768]{1,0:T(8,128)}, f32[1088,768]{1,0:T(8,128)S(1)}, u32[]{:S(2)}) copy-start(f32[1088,768]{1,0:T(8,128)S(1)} %get-tuple-element.301) | copy-start | bytes 10027012
  172.1 42.4 %copy-start.45 = (f32[1088]{0:T(1024)}, f32[1088]{0:T(1024)S(1)}, u32[]{:S(2)}) copy-start(f32[1088]{0:T(1024)S(1)} %add_rsqrt_fusion) | copy-start | bytes 13060
  172.1 42.4 %slice-start.2 = ((s8[4718592]{0:T(1024)(128)(4,1)}), s8[4194304]{0:T(1024)(128)(4,1)S(1)}, s32[]{:S(2)}) async-start(s8[4718592]{0:T(1024)(128)(4,1)} %bitcast.275), calls=%async_computation.32 | async-start | bytes 8388608
  237.1 17.2 %all-to-all-start.1 = ((bf16[8,32,768]{2,1,0:T(8,128)(2,1)}), bf16[8,32,768]{2,1,0:T(8,128)(2,1)}, u32[]{:S(2)}, u32[]{:S(2)}) async-start(bf16[8,32,768]{2,1,0:T(8,128)(2,1)} %bitcast.268), calls=%async_computation.1 | async-start | bytes 786432 | tf_op jit(solution)/shard_map/all_to_all | solution.py:323
  243.1 451.7 %reduce-scatter.40.cloned.1.call-start = ((), (), s32[]{:S(2)}) async-start(), calls=%async_computation.27 | async-start | bytes 294912
  371.9 15.9 %all-to-all-start.2 = ((bf16[8,32,768]{2,1,0:T(8,128)(2,1)}), bf16[8,32,768]{2,1,0:T(8,128)(2,1)}, u32[]{:S(2)}, u32[]{:S(2)}) async-start(bf16[8,32,768]{2,1,0:T(8,128)(2,1)} %bitcast.269), calls=%async_computation.2 | async-start | bytes 786432 | tf_op jit(solution)/shard_map/all_to_all | solution.py:351
  376.0 320.3 %reduce-scatter.42.cloned.1.call-start = ((), (), s32[]{:S(2)}) async-start(), calls=%async_computation.28 | async-start | bytes 294912
  377.6 320.0 %reduce-scatter.28.cloned.1.call-start = ((), (), s32[]{:S(2)}) async-start(), calls=%async_computation.21 | async-start | bytes 589824 | tf_op jit(solution)/shard_map/reduce_scatter | solution.py:413
  385.6 312.1 %reduce-scatter.20.cloned.1.call-start = ((), (), s32[]{:S(2)}) async-start(), calls=%async_computation.17 | async-start | bytes 1327104 | tf_op jit(solution)/shard_map/reduce_scatter | solution.py:413
  439.5 258.2 %reduce-scatter.26.cloned.1.call-start = ((), (), s32[]{:S(2)}) async-start(), calls=%async_computation.20 | async-start | bytes 1769472 | tf_op jit(solution)/shard_map/reduce_scatter | solution.py:413
  442.4 322.4 %reduce-scatter.30.cloned.1.call-start = ((), (), s32[]{:S(2)}) async-start(), calls=%async_computation.22 | async-start | bytes 2359296 | tf_op jit(solution)/shard_map/reduce_scatter | solution.py:413
  449.2 386.0 %reduce-scatter.34.cloned.1.call-start = ((), (), s32[]{:S(2)}) async-start(), calls=%async_computation.24 | async-start | bytes 2359296 | tf_op jit(solution)/shard_map/reduce_scatter | solution.py:413
  455.2 450.0 %reduce-scatter.36.cloned.1.call-start = ((), (), s32[]{:S(2)}) async-start(), calls=%async_computation.25 | async-start | bytes 2359296 | tf_op jit(solution)/shard_map/reduce_scatter | solution.py:413
  461.9 525.1 %reduce-scatter.18.cloned.1.call-start = ((), (), s32[]{:S(2)}) async-start(), calls=%async_computation.16 | async-start | bytes 3981312 | tf_op jit(solution)/shard_map/reduce_scatter | solution.py:413
  475.6 158.0 %copy-start.40 = (f32[1088]{0:T(1024)S(1)}, f32[1088]{0:T(1024)}, u32[]{:S(2)}) copy-start(f32[1088]{0:T(1024)} %copy-done.39) | copy-start | bytes 13060
  643.9 434.1 %reduce-scatter.38.cloned.1.call-start = ((), (), s32[]{:S(2)}) async-start(), calls=%async_computation.26 | async-start | bytes 4718592 | tf_op jit(solution)/shard_map/reduce_scatter | solution.py:413
  653.6 523.7 %reduce-scatter.22.cloned.1.call-start = ((), (), s32[]{:S(2)}) async-start(), calls=%async_computation.18 | async-start | bytes 5308416 | tf_op jit(solution)/shard_map/reduce_scatter | solution.py:413
  665.5 610.9 %reduce-scatter.24.cloned.1.call-start = ((), (), s32[]{:S(2)}) async-start(), calls=%async_computation.19 | async-start | bytes 5308416 | tf_op jit(solution)/shard_map/reduce_scatter | solution.py:413
  676.1 722.0 %reduce-scatter.32.cloned.1.call-start = ((), (), s32[]{:S(2)}) async-start(), calls=%async_computation.23 | async-start | bytes 7077888 | tf_op jit(solution)/shard_map/reduce_scatter | solution.py:413
  689.3 708.9 %copy-start.51 = (f32[1088]{0:T(1024)S(1)}, f32[1088]{0:T(1024)}, u32[]{:S(2)}) copy-start(f32[1088]{0:T(1024)} %copy-done.50) | copy-start | bytes 13060
  689.3 804.7 %all-reduce.15.cloned.1.call-start = ((), (), s32[]{:S(2)}) async-start(), calls=%async_computation.29 | async-start | bytes 8257536 | tf_op jit(solution)/shard_map/psum | solution.py:416
  (65 other events, 670.5 us)
Sparse Core Ops, SparseCore 0:
  369.4 60.8 reduce-scatter.39
  434.1 60.2 reduce-scatter.41
  498.3 60.8 reduce-scatter.27
  563.5 63.1 reduce-scatter.19
  630.9 63.8 reduce-scatter.25
  698.2 66.5 reduce-scatter.29
  768.3 66.7 reduce-scatter.33
  838.7 66.5 reduce-scatter.35
  908.9 78.1 reduce-scatter.17
  990.5 87.4 reduce-scatter.37
  1082.1 95.1 reduce-scatter.21
  1181.2 95.1 reduce-scatter.23
  1280.4 117.7 reduce-scatter.31
  1401.5 85.6 all-reduce.14
where the time goes:
time: 1520 us
  waiting for transfers between devices  706 us (46%)
  matrix products  486 us (32%)
  local copies, waits for them, and re-layouts  138 us (9%)
  other arithmetic  98.6 us (6%)
  blocking collectives  48.9 us (3%)
  between operations  19.1 us (1%)
  starting transfers between devices  18.8 us (1%)
    reduce_scatter x11, waiting for transfers between devices, shards(): lax.psum_scatter(for_sending(local_grads), 'wide', scatter_dimension=0, t...  701 us
    dot_general x41, matrix products, contract_last(): lax.dot_general(left, right, (((1,), (1,)), ((), ())), preferred_element_...  130 us
    dot_general x29, matrix products, matmul(): return jnp.dot(left, right, preferred_element_type=jnp.float32)  113 us
    dot_general x29, matrix products, contract_rows(): lax.dot_general(left, right, (((0,), (0,)), ((), ())), preferred_element_...  96.7 us
    unnamed x163, local copies, waits for them, and re-layouts  42.4 us
    unnamed x1, blocking collectives  36.6 us
  transfers between devices with their start and end apart: 17, of which 10 were waited for; matrix products, arithmetic and copies ran while one was open for 37% of the time, Pallas kernels for 0%

commit v1 on v0

--- a/solution.py
+++ b/solution.py
@@ -4,6 +4,8 @@
 import jax
 import jax.numpy as jnp
 from jax import lax
+from jax.experimental import pallas as pl
+from jax.experimental.pallas import tpu as pltpu
 from jax.sharding import PartitionSpec as P
 
 D = 768
@@ -60,43 +62,207 @@
     return grad_after * sigma * (1.0 + before * (1.0 - sigma))
 
 
-def to_heads(array):
-    return array.reshape(array.shape[0], HEADS, HEAD_DIM).transpose(1, 0, 2)
-
-
-def from_heads(array):
-    return array.transpose(1, 0, 2).reshape(array.shape[1], HEADS * HEAD_DIM)
-
-
-def attend(query, keys, values, keep_keys, scale):
-
-    def single(inputs):
-        head_query, head_keys, head_values = inputs
-        scores = jnp.where(keep_keys[None, :], contract_last(head_query, head_keys) * scale, -1e30)
-        top = jnp.max(scores, axis=-1, keepdims=True)
-        total = jnp.sum(jnp.exp(scores - top), axis=-1, keepdims=True)
-        logsum = top + jnp.log(total)
-        probs = jnp.exp(scores - logsum).astype(jnp.bfloat16)
-        return (matmul(probs, head_values).astype(jnp.bfloat16), logsum[:, 0])
-
-    return lax.map(single, (query, keys, values))
-
-
-def attend_back(query, keys, values, logsum, grad_mixed, keep_keys, scale):
-
-    def single(inputs):
-        head_query, head_keys, head_values, head_logsum, head_grad = inputs
-        scores = jnp.where(keep_keys[None, :], contract_last(head_query, head_keys) * scale, -1e30)
-        probs = jnp.exp(scores - head_logsum[:, None])
-        grad_probs = contract_last(head_grad, head_values)
-        across = jnp.sum(probs * grad_probs, axis=-1, keepdims=True)
-        grad_scores = (probs * (grad_probs - across)).astype(jnp.bfloat16)
-        grad_query = (matmul(grad_scores, head_keys) * scale).astype(jnp.bfloat16)
-        grad_keys = (contract_rows(grad_scores, head_query) * scale).astype(jnp.bfloat16)
-        grad_values = contract_rows(probs.astype(jnp.bfloat16), head_grad).astype(jnp.bfloat16)
-        return (grad_query, grad_keys, grad_values)
-
-    return lax.map(single, (query, keys, values, logsum, grad_mixed))
+PAIRS = 6
+VM=60*1024*1024
+
+def nt(a,b): return lax.dot_general(a,b,(((1,),(1,)),((),())),preferred_element_type=jnp.float32)
+def nn(a,b): return jnp.dot(a,b,preferred_element_type=jnp.float32)
+def tn(a,b): return lax.dot_general(a,b,(((0,),(0,)),((),())),preferred_element_type=jnp.float32)
+
+def fwd_kernel(QB, len_ref, q_ref, k_ref, v_ref, o_ref, lse_ref):
+    length=len_ref[0]
+    low=lax.broadcasted_iota(jnp.int32,(1,128),1)<64
+    bias=jnp.where(lax.broadcasted_iota(jnp.int32,(1,SEQ),1)<length,0.0,-1e30).astype(jnp.float32)
+    k=k_ref[...]; v=v_ref[...]
+    one=jnp.ones((),v.dtype); zero=jnp.zeros((),v.dtype)
+    vs=(jnp.where(low,v,one),jnp.where(low,one,v))
+    for b in range(SEQ//QB):
+        rows=pl.ds(b*QB,QB)
+        q=q_ref[rows,:]
+        outs=[];lses=[]
+        for h in range(2):
+            qh=jnp.where(low,q,zero) if h==0 else jnp.where(low,zero,q)
+            s=nt(qh,k)+bias
+            top=jnp.max(s,axis=1,keepdims=True)
+            p=jnp.exp(s-top).astype(jnp.bfloat16)
+            o=nn(p,vs[h])
+            total=pltpu.roll(o,64,1)
+            outs.append(o/total)
+            lses.append(top+jnp.log(total))
+        o_ref[rows,:]=jnp.where(low,outs[0],outs[1]).astype(jnp.bfloat16)
+        lse_ref[rows,:]=jnp.where(low,lses[0],lses[1])
+
+def attend(joint,length,QB=272):
+    spec=lambda off: pl.BlockSpec((SEQ,128),lambda i,off=off:(0,i+off))
+    return pl.pallas_call(partial(fwd_kernel,QB),
+        grid=(PAIRS,),
+        in_specs=[pl.BlockSpec(memory_space=pltpu.SMEM),spec(0),spec(6),spec(12)],
+        out_specs=[spec(0),spec(0)],
+        out_shape=[jax.ShapeDtypeStruct((SEQ,D),jnp.bfloat16),jax.ShapeDtypeStruct((SEQ,D),jnp.float32)],
+        compiler_params=pltpu.CompilerParams(vmem_limit_bytes=VM),
+        cost_estimate=pl.CostEstimate(flops=4*SEQ*SEQ*D,bytes_accessed=SEQ*D*12,transcendentals=SEQ*SEQ*12),
+        name='attend')(length,joint,joint,joint)
+
+def bwd_kernel(KB,MODE,len_ref,q_ref,k_ref,v_ref,do_ref,o_ref,lse_ref,dq_ref,dk_ref,dv_ref,ds_ref):
+    length=len_ref[0]
+    low=lax.broadcasted_iota(jnp.int32,(1,128),1)<64
+    q=q_ref[...]; do=do_ref[...]
+    zero=jnp.zeros((),q.dtype)
+    prod=do.astype(jnp.float32)*o_ref[...].astype(jnp.float32)
+    prodT=prod.T
+    lseT=lse_ref[...].T
+    deltas=(jnp.sum(prodT[:64],axis=0,keepdims=True),jnp.sum(prodT[64:],axis=0,keepdims=True))
+    lses=(lseT[0:1],lseT[64:65])
+    for b in range(SEQ//KB):
+        rows=pl.ds(b*KB,KB)
+        k=k_ref[rows,:]; v=v_ref[rows,:]
+        bias=jnp.where(lax.broadcasted_iota(jnp.int32,(KB,1),0)+b*KB<length,0.0,-1e30).astype(jnp.float32)
+        dks=[];dvs=[]
+        for h in range(2):
+            pick=(lambda a: jnp.where(low,a,zero)) if h==0 else (lambda a: jnp.where(low,zero,a))
+            s=nt(pick(k),q)+bias
+            p=jnp.exp(s-lses[h])
+            dp=nt(pick(v),do)
+            ds=(p*(dp-deltas[h])).astype(jnp.bfloat16)
+            dvs.append(nn(p.astype(jnp.bfloat16),do))
+            dks.append(nn(ds,q))
+            ds_ref[h,rows,:]=ds
+        dk_ref[rows,:]=jnp.where(low,dks[0],dks[1]).astype(jnp.bfloat16)
+        dv_ref[rows,:]=jnp.where(low,dvs[0],dvs[1]).astype(jnp.bfloat16)
+    if MODE=='tn':
+        dq=[tn(ds_ref[h],k_ref[...]) for h in range(2)]
+        dq_ref[...]=(jnp.where(low,dq[0],dq[1])*0.125).astype(jnp.bfloat16)
+    else:
+        kT=k_ref[...].astype(jnp.float32).T.astype(jnp.bfloat16)
+        dqT=jnp.concatenate([nn(kT[64*h:64*h+64],ds_ref[h]) for h in range(2)],axis=0)
+        dq_ref[...]=(dqT.T*0.125).astype(jnp.bfloat16)
+
+def attend_back(joint,do,o,lse,length,KB=544,MODE='kt'):
+    spec=lambda off: pl.BlockSpec((SEQ,128),lambda i,off=off:(0,i+off))
+    return pl.pallas_call(partial(bwd_kernel,KB,MODE),
+        grid=(PAIRS,),
+        in_specs=[pl.BlockSpec(memory_space=pltpu.SMEM),spec(0),spec(6),spec(12),spec(0),spec(0),spec(0)],
+        out_specs=[spec(0)]*3,
+        out_shape=[jax.ShapeDtypeStruct((SEQ,D),jnp.bfloat16)]*3,
+        scratch_shapes=[pltpu.VMEM((2,SEQ,SEQ),jnp.bfloat16)],
+        compiler_params=pltpu.CompilerParams(vmem_limit_bytes=VM),
+        cost_estimate=pl.CostEstimate(flops=10*SEQ*SEQ*D,bytes_accessed=SEQ*D*18,transcendentals=SEQ*SEQ*12),
+        name='attend_back')(length,joint,joint,joint,do,o,lse)
+
+
+def add_up(terms):
+    total = terms[0].astype(jnp.float32)
+    for term in terms[1:]:
+        total = total + term.astype(jnp.float32)
+    return total
+
+
+def swap(array, axis, mask):
+    count = lax.axis_size(axis)
+    return lax.ppermute(array, axis, [(i, i ^ mask) for i in range(count)])
+
+
+def bit(label):
+    return lax.axis_index(label[0]) // label[1] % 2
+
+
+def behind(value, *others):
+    return lax.optimization_barrier((value,) + others)[0]
+
+
+class Flow:
+    def __init__(self, whole):
+        wide, narrow = lax.axis_size("wide"), lax.axis_size("narrow")
+        labels = [("wide", 1 << b) for b in reversed(range(wide.bit_length() - 1))]
+        labels += [("narrow", 1 << b) for b in reversed(range(narrow.bit_length() - 1))]
+        rows = whole.shape[0] // (wide * narrow)
+        first = [("narrow", 1 << b) for b in range(1, narrow.bit_length() - 1)] + [("wide", 1)]
+        cut = whole.shape[1] // 256 * 128
+        whole = whole.reshape((2,) * len(labels) + (rows,) + whole.shape[1:])
+        self.lanes = [
+            {"cols": (0, cut), "order": first},
+            {"cols": (cut, whole.shape[-1]), "order": first[::-1]},
+        ]
+        self.labels = labels
+        self.terms = [whole]
+        self.count = len(first)
+        self.steps = self.run()
+
+    def step(self):
+        return next(self.steps)
+
+    def take(self, term, labels, picks):
+        labels = list(labels)
+        for label, value in picks:
+            term = lax.dynamic_index_in_dim(term, value, labels.index(label), keepdims=False)
+            labels.remove(label)
+        return term
+
+    def halve(self, terms, labels, label):
+        mine = bit(label)
+        sent = add_up([self.take(t, labels, [(label, 1 - mine)]) for t in terms])
+        got = swap(sent.astype(jnp.bfloat16), *label)
+        kept = [self.take(t, labels, [(label, mine)]) for t in terms]
+        return kept + [got], [l for l in labels if l != label], got
+
+    def run(self):
+        terms, labels, got = self.halve(self.terms, self.labels, ("narrow", 1))
+        yield (got,)
+        lanes = []
+        for lane in self.lanes:
+            lanes.append(([t[..., lane["cols"][0] : lane["cols"][1]] for t in terms], labels))
+        for turn in range(self.count):
+            arrived = []
+            for i, lane in enumerate(self.lanes):
+                terms, labels, got = self.halve(*lanes[i], lane["order"][turn])
+                lanes[i] = (terms, labels)
+                arrived.append(got)
+            yield tuple(arrived)
+        labels = lanes[0][1]
+        axis = labels[0][0]
+        arrived = []
+        for pick in range(1 << len(labels)):
+            mask = sum(label[1] for i, label in enumerate(labels) if pick >> i & 1)
+            picks = [(l, (1 - bit(l)) if mask & l[1] else bit(l)) for l in labels]
+            part = jnp.concatenate(
+                [
+                    add_up([self.take(t, labels, picks) for t in terms]).astype(jnp.bfloat16)
+                    for terms, labels in lanes
+                ],
+                axis=-1,
+            )
+            if mask:
+                arrived.append(swap(part, axis, mask))
+            else:
+                own = part
+        yield tuple(arrived)
+        share = add_up([own] + arrived).astype(jnp.bfloat16)
+        count = lax.axis_size("narrow")
+        stack = share[None]
+        mask = count // 2
+        while mask:
+            got = swap(stack, "narrow", mask)
+            yield (got,)
+            low = bit(("narrow", mask)) == 0
+            stack = jnp.concatenate(
+                [jnp.where(low, stack, got), jnp.where(low, got, stack)], axis=0
+            )
+            mask //= 2
+        half = int(math.log2(count))
+        shape = stack.shape[1:]
+        stack = stack.reshape((2,) * half + shape)
+        stack = stack.transpose(tuple(reversed(range(half))) + (half, half + 1))
+        self.result = stack.reshape((count,) + shape)
+        yield ()
+
+
+def small_sum(rows):
+    narrow, wide = lax.axis_size("narrow"), lax.axis_size("wide")
+    low = rows.astype(jnp.bfloat16)
+    low = add_up([low] + [swap(low, "narrow", m) for m in range(1, narrow)]).astype(jnp.bfloat16)
+    place = lax.axis_index("wide")
+    parts = [lax.dynamic_index_in_dim(low, place ^ m, 0, keepdims=False) for m in range(wide)]
+    return add_up(parts[:1] + [swap(parts[m], "wide", m) for m in range(1, wide)])
 
 
 def diffusion_pass(rows, latent, noise_part, steps, live, weights):
@@ -187,17 +353,24 @@
         jnp.bfloat16
     )
     grad_finmod = jnp.concatenate([grad_last, grad_scale_b], axis=-1).astype(jnp.bfloat16)
-    block_mod_grad = jnp.einsum(
-        "rsw,rsv->wv", acted, grad_modul, preferred_element_type=jnp.float32
-    )
     final_mod_grad = jnp.einsum(
         "rsw,rsv->wv", acted, grad_finmod, preferred_element_type=jnp.float32
     )
+    flow_one = Flow(
+        jnp.concatenate(
+            [g.astype(jnp.bfloat16) for g in (final_mod_grad, block_reduce_grad, block_expand_grad)],
+            axis=1,
+        )
+    )
+    grad_modul = behind(grad_modul, *flow_one.step())
+    one = flow_one.step()
     grad_acted = jnp.einsum(
         "rsv,wv->rsw", grad_modul, block_mod, preferred_element_type=jnp.float32
     ) + jnp.einsum("rsv,wv->rsw", grad_finmod, final_mod, preferred_element_type=jnp.float32)
     grad_cond = silu_back(cond_all, grad_acted)
     grad_timed = grad_cond.astype(jnp.bfloat16)
+    grad_embed = jnp.sum(grad_cond, axis=0).astype(jnp.bfloat16)
+    grad_rows = contract_last(grad_embed, cond_proj)
     time_second_grad = jnp.einsum(
         "rsw,rsv->wv", first_low, grad_timed, preferred_element_type=jnp.float32
     )
@@ -208,24 +381,30 @@
     time_first_grad = jnp.einsum(
         "rsf,rsw->fw", sinus, grad_first, preferred_element_type=jnp.float32
     )
-    grad_embed = jnp.sum(grad_cond, axis=0).astype(jnp.bfloat16)
     cond_proj_grad = contract_rows(rows, grad_embed)
-    grad_rows = contract_last(grad_embed, cond_proj)
-    return (
-        guess,
-        grad_rows,
-        (
-            input_proj_grad,
-            cond_proj_grad,
-            time_first_grad,
-            time_second_grad,
-            block_mod_grad,
-            block_expand_grad,
-            block_reduce_grad,
-            final_mod_grad,
-            final_proj_grad,
-        ),
-    )
+    acted_later = behind(acted, *one)
+    one = flow_one.step()
+    block_mod_grad = jnp.einsum(
+        "rsw,rsv->wv", acted_later, grad_modul, preferred_element_type=jnp.float32
+    )
+    total = lax.axis_size("wide") * lax.axis_size("narrow")
+
+    def chunked(grad):
+        return grad.astype(jnp.bfloat16).reshape(total, -1, grad.shape[1])
+
+    mixed_rows = jnp.concatenate([chunked(cond_proj_grad), chunked(time_first_grad)], axis=1)
+    flow_two = Flow(
+        jnp.concatenate(
+            [
+                block_mod_grad.astype(jnp.bfloat16),
+                time_second_grad.astype(jnp.bfloat16),
+                mixed_rows.reshape(-1, width),
+            ],
+            axis=1,
+        )
+    )
+    two = flow_two.step()
+    return (guess, grad_rows, (input_proj_grad, final_proj_grad), (flow_one, one), (flow_two, two))
 
 
 def shards(
@@ -273,11 +452,10 @@
     first_normed, first_inverse = normalize(image)
     first_in = (first_normed * first_gain + first_shift).astype(jnp.bfloat16)
     joint = matmul(first_in, joint_weight)
-    query = to_heads((joint[:, :D] + query_value_bias[:D]).astype(jnp.bfloat16))
-    keys = to_heads(joint[:, D : 2 * D].astype(jnp.bfloat16))
-    values = to_heads((joint[:, 2 * D :] + query_value_bias[D:]).astype(jnp.bfloat16))
-    mixed_heads, logsum = attend(query, keys, values, keep_keys, scale)
-    mixed = from_heads(mixed_heads)
+    joint_bias = jnp.concatenate([query_value_bias[:D], jnp.zeros((D,), jnp.float32), query_value_bias[D:]])
+    joint_scale = jnp.where(jnp.arange(3 * D) < D, scale, 1.0)
+    joint_low = ((joint + joint_bias).astype(jnp.bfloat16) * joint_scale.astype(jnp.bfloat16))
+    mixed, logsum = attend(joint_low, length[None])
     branch = matmul(mixed, output_weight) + output_bias
     middle = image + branch
     second_normed, second_inverse = normalize(middle)
@@ -340,7 +518,7 @@
     first_rank = (place_wide - deal_start[sources]) % wide_count
     arrived = jnp.maximum((source_count - first_rank + wide_count - 1) // wide_count, 0)
     live = (jnp.arange(capacity)[None, :] < arrived[:, None]).astype(jnp.float32).reshape(-1)
-    guess, grad_rows, head_grads = diffusion_pass(
+    guess, grad_rows, head_smalls, (flow_one, one), (flow_two, two) = diffusion_pass(
         got_rows.reshape(-1, D),
         got_latent.reshape(-1, TOKEN_DIM),
         added_noise,
@@ -359,11 +537,27 @@
     head_to_tokens = padded[target].astype(jnp.float32)
     grad_out = (cotangent.astype(jnp.float32) + head_to_tokens) * keep_rows
     grad_feed = grad_out.astype(jnp.bfloat16)
+    grad_feed = behind(grad_feed, *one, *two)
+    one = flow_one.step()
+    two = flow_two.step()
     reduce_weight_grad = contract_rows(active_low, grad_feed)
     reduce_bias_grad = jnp.sum(grad_feed.astype(jnp.float32), axis=0)
     grad_active = contract_last(grad_feed, reduce_weight)
     grad_hidden = gelu_back(grad_active)[0].astype(jnp.bfloat16)
+    grad_hidden = behind(grad_hidden, *one, *two)
+    one = flow_one.step()
+    two = flow_two.step()
     expand_weight_grad = contract_rows(second_in, grad_hidden)
+    total = wide_count * narrow_count
+
+    def low(grad):
+        return grad.astype(jnp.bfloat16)
+
+    parts = low(reduce_weight_grad).reshape(total, -1, D)
+    piece = D // total
+    ratio = parts.shape[1] // piece
+    reduce_wide = jnp.concatenate([parts[:, i * piece : (i + 1) * piece] for i in range(ratio)], axis=2)
+    flow_feed = Flow(jnp.concatenate([low(expand_weight_grad), reduce_wide.reshape(D, -1)], axis=1))
     expand_bias_grad = jnp.sum(grad_hidden.astype(jnp.float32), axis=0)
     grad_second = contract_last(grad_hidden, expand_weight)
     second_gain_grad = jnp.sum(grad_second * second_normed, axis=0)
@@ -372,16 +566,28 @@
         grad_second * second_gain, second_normed, second_inverse
     )
     grad_branch = grad_middle.astype(jnp.bfloat16)
+    grad_branch = behind(grad_branch, *one, *two)
+    one = flow_one.step()
+    two = flow_two.step()
+    feed = flow_feed.step()
     output_weight_grad = contract_rows(mixed, grad_branch)
     output_bias_grad = jnp.sum(grad_branch.astype(jnp.float32), axis=0)
-    grad_mixed = to_heads(contract_last(grad_branch, output_weight).astype(jnp.bfloat16))
+    grad_mixed = contract_last(grad_branch, output_weight).astype(jnp.bfloat16)
+    grad_mixed = behind(grad_mixed, *feed)
+    feed = flow_feed.step()
     grad_query, grad_keys, grad_values = attend_back(
-        query, keys, values, logsum, grad_mixed, keep_keys, scale
-    )
-    grad_query = from_heads(grad_query)
-    grad_values = from_heads(grad_values)
-    grad_joint = jnp.concatenate([grad_query, from_heads(grad_keys), grad_values], axis=1)
+        joint_low, grad_mixed, mixed, logsum, length[None]
+    )
+    grad_joint = jnp.concatenate([grad_query, grad_keys, grad_values], axis=1)
+    grad_joint = behind(grad_joint, *one, *two, *feed)
+    one = flow_one.step()
+    two = flow_two.step()
+    feed = flow_feed.step()
     joint_weight_grad = contract_rows(first_in, grad_joint)
+    flow_last = Flow(jnp.concatenate([low(joint_weight_grad), low(output_weight_grad)], axis=1))
+    last = flow_last.step()
+    grad_joint = behind(grad_joint, *last)
+    last = flow_last.step()
     query_value_bias_grad = jnp.concatenate(
         [
             jnp.sum(grad_query.astype(jnp.float32), axis=0),
@@ -394,28 +600,80 @@
     tokens_gradient = grad_middle + normalize_back(
         grad_first * first_gain, first_normed, first_inverse
     )
-    local_grads = (
+    (input_proj_grad, final_proj_grad) = head_smalls
+    width = cond_proj.shape[1]
+    flows = (flow_one, flow_two, flow_feed, flow_last)
+    for flow in flows:
+        for unused in flow.steps:
+            pass
+    one_sum, two_sum, feed_sum, last_sum = [flow.result for flow in flows]
+
+    def full(rows):
+        return rows.reshape(-1, rows.shape[-1]).astype(jnp.float32)
+
+    final_mod_out = full(one_sum[..., : 2 * width])
+    block_reduce_out = full(one_sum[..., 2 * width : 3 * width])
+    block_expand_out = full(one_sum[..., 3 * width : 4 * width])
+    block_mod_out = full(two_sum[..., : 3 * width])
+    time_second_out = full(two_sum[..., 3 * width : 4 * width])
+    cut = D // total
+    cond_out = full(two_sum[:, :cut, 4 * width :])
+    time_first_out = full(two_sum[:, cut:, 4 * width :])
+    hidden_width = expand_weight.shape[1]
+    expand_out = full(feed_sum[..., :hidden_width])
+    wide_parts = feed_sum[..., hidden_width:]
+    reduce_out = full(
+        jnp.concatenate([wide_parts[..., i * D : (i + 1) * D] for i in range(ratio)], axis=1)
+    )
+    joint_out = full(last_sum[..., : 3 * D])
+    output_out = full(last_sum[..., 3 * D :])
+    smalls = (
         first_gain_grad,
         first_shift_grad,
-        joint_weight_grad,
         query_value_bias_grad,
-        output_weight_grad,
         output_bias_grad,
         second_gain_grad,
         second_shift_grad,
-        expand_weight_grad,
         expand_bias_grad,
-        reduce_weight_grad,
         reduce_bias_grad,
-    ) + tuple(head_grads)
-    shares = jax.tree.map(
-        lambda part: part.astype(jnp.float32),
-        lax.psum_scatter(for_sending(local_grads), "wide", scatter_dimension=0, tiled=True),
-    )
-    totals = jax.tree.map(
-        lambda part: part.astype(jnp.float32), lax.psum(for_sending(shares), "narrow")
-    )
-    return (block_output, guess, spread, tokens_gradient) + tuple(totals)
+        input_proj_grad,
+        final_proj_grad,
+    )
+    packed = jnp.concatenate([g.reshape(wide_count, -1) for g in smalls], axis=1)
+    small = small_sum(packed)
+    outs = []
+    at = 0
+    for g in smalls:
+        size = g.size // wide_count
+        outs.append(small[at : at + size].reshape((-1,) + g.shape[1:]))
+        at += size
+    return (
+        block_output,
+        guess,
+        spread,
+        tokens_gradient,
+        outs[0],
+        outs[1],
+        joint_out,
+        outs[2],
+        output_out,
+        outs[3],
+        outs[4],
+        outs[5],
+        expand_out,
+        outs[6],
+        reduce_out,
+        outs[7],
+        outs[8],
+        cond_out,
+        time_first_out,
+        time_second_out,
+        block_mod_out,
+        block_expand_out,
+        block_reduce_out,
+        final_mod_out,
+        outs[9],
+    )
 
 
 def solution(mesh):

time: 1520 us -> 783 us (0.52)
  waiting for transfers between devices: 706 us -> 76.2 us
  matrix products: 486 us -> 268 us
  Pallas kernels: 0 us -> 67.9 us
  starting transfers between devices: 18.8 us -> 85.7 us
  other arithmetic: 98.6 us -> 151 us
  blocking collectives: 48.9 us -> 0 us
  local copies, waits for them, and re-layouts: 138 us -> 122 us
    reduce_scatter x11 -> x0, waiting for transfers between devices: 701 us -> none  [shards(): lax.psum_scatter(for_sending(local_grads), 'wide', scatter_dimension=0, t...]
    dot_general x41 -> x5, matrix products: 130 us -> 45.5 us  [contract_last(): lax.dot_general(left, right, (((1,), (1,)), ((), ())), preferred_element_...]
    ppermute x0 -> x50, waiting for transfers between devices: none -> 68.2 us  [swap(): return lax.ppermute(array, axis, [(i, i ^ mask) for i in range(count)])]
    ppermute x0 -> x50, starting transfers between devices: none -> 68.1 us  [swap(): return lax.ppermute(array, axis, [(i, i ^ mask) for i in range(count)])]
    pallas_call x0 -> x2, Pallas kernels: none -> 67.9 us  [the longest x1 41.9 us: attend_back(): pl.pallas_call(partial(bwd_kernel, KB, MODE), grid=(PAIRS,), in_specs=[pl...]
    dot_general x29 -> x5, matrix products: 96.7 us -> 32.1 us  [contract_rows(): lax.dot_general(left, right, (((0,), (0,)), ((), ())), preferred_element_...]
    dot_general x29 -> x5, matrix products: 113 us -> 66.7 us  [matmul(): return jnp.dot(left, right, preferred_element_type=jnp.float32)]
    unnamed x1 -> x0, blocking collectives: 36.6 us -> none
  transfers between devices with their start and end apart: 17 -> 53, of which waited for: 10 -> 22; matrix products, arithmetic and copies ran while one was open for 37% -> 47% of each run, Pallas kernels for 0% -> 9%
where the time goes in v1:
time: 783 us; the launch traced here: 776 us
  matrix products  268 us (34%)
  other arithmetic  151 us (19%)
  local copies, waits for them, and re-layouts  122 us (16%)
  starting transfers between devices  85.7 us (11%)
  waiting for transfers between devices  76.2 us (10%)
  Pallas kernels  67.9 us (9%)
    ppermute x50, waiting for transfers between devices, swap(): return lax.ppermute(array, axis, [(i, i ^ mask) for i in range(count)])  68.2 us
    ppermute x50, starting transfers between devices, swap(): return lax.ppermute(array, axis, [(i, i ^ mask) for i in range(count)])  68.1 us
    dot_general x5, matrix products, matmul(): return jnp.dot(left, right, preferred_element_type=jnp.float32)  66.7 us
    dot_general x5, matrix products, contract_last(): lax.dot_general(left, right, (((1,), (1,)), ((), ())), preferred_element_...  45.5 us
    pallas_call x1, Pallas kernels, attend_back(): pl.pallas_call(partial(bwd_kernel, KB, MODE), grid=(PAIRS,), in_specs=[pl...  41.9 us
    dot_general x5, matrix products, contract_rows(): lax.dot_general(left, right, (((0,), (0,)), ((), ())), preferred_element_...  32.1 us
    pallas_call x1, Pallas kernels, attend(): pl.pallas_call(partial(fwd_kernel, QB), grid=(PAIRS,), in_specs=[pl.Block...  26 us
    unnamed x221, local copies, waits for them, and re-layouts  25.7 us
  transfers between devices with their start and end apart: 53, of which 22 were waited for; matrix products, arithmetic and copies ran while one was open for 47% of the time, Pallas kernels for 9%

profile of v1, /device:TPU:0, one launch (start us, length us, event | category | flops | bytes accessed | tf_op | source)
XLA Modules:
  0.0 775.8 jit_solution(4628148831245329425)
XLA Ops:
  51.2 26.0 %attend.1 = (bf16[1088,768]{1,0:T(8,128)(2,1)}, f32[1088,768]{1,0:T(8,128)}) custom-call(s32[1]{0:T(128)} %add_shard_map.6.len_ref, bf16[1088,2304]{1,0:T(8,128)(2,1)} %fusion.7.q_ref.k_ref.v_ref, bf16[1088,2304]{1,0:T(8,128)(2,1)} %fusion.7.q_ref.k_ref.v_ref, bf16[1088,2304]{1,0:T(8,128)(2,1)} %fusion.7.q_ref.k_ref.v_ref), custom_call_target="tpu_custom_call" | custom-call | flops 3636461568 | bytes 10027008 | tf_op jit(solution)/shard_map/attend/pallas_call | solution.py:97
  85.8 40.5 %multiply_convert_fusion = (bf16[1088,3072]{1,0:T(8,128)(2,1)S(1)}, f32[1088,3072]{1,0:T(8,128)}, f32[1088,3072]{1,0:T(8,128)}) fusion(f32[3072]{0:T(1024)} %param.46, bf16[768,3072]{1,0:T(8,128)(2,1)} %param.45, f32[1088,768]{1,0:T(8,128)} %copy-done.10, f32[768]{0:T(1024)} %param.44, f32[768]{0:T(1024)} %param.43, f32[1088]{0:T(1024)} %add_rsqrt_fusion, ...), kind=kOutput, calls=%fused_computation.10 | convolution fusion | flops 5358600192 | bytes 41511424 | tf_op jit(solution)/shard_map/dot_general | solution.py:31
  126.3 12.2 %fusion.38 = (f32[]{:T(128)}, f32[]{:T(128)}, bf16[1088,768]{1,0:T(8,128)(2,1)}) fusion(f32[1088,768]{1,0:T(8,128)S(1)} %copy-done.96, f32[1088]{0:T(1024)S(1)} %fusion.146, f32[1088,768]{1,0:T(8,128)S(1)} %copy-done.11, f32[768]{0:T(1024)S(1)} %copy-done.92, bf16[1088,3072]{1,0:T(8,128)(2,1)S(1)} %get-tuple-element.178, bf16[3072,768]{1,0:T(8,128)(2,1)} %param.47), kind=kOutput, calls=%fused_computation.113 | convolution fusion | flops 5142183936 | bytes 19766536 | tf_op jit(solution)/shard_map/dot_general | solution.py:31
  140.0 11.3 %fusion.80 = (bf16[4,256,128]{2,1,0:T(8,128)(2,1)S(1)}, bf16[4,256,128]{2,1,0:T(8,128)(2,1)S(1)}) fusion(f32[128]{0:T(128)S(1)} %copy-done.88, f32[4,256]{1,0:T(4,128)S(1)} %copy-done.76), kind=kLoop, calls=%fused_computation.202 | loop fusion | flops 393216 | bytes 528896 | tf_op jit(solution)/shard_map/convert.115
  157.7 9.5 %scatter_custom_fusion.1 = bf16[257,768]{1,0:T(8,128)(2,1)} fusion(s32[1088]{0:T(1024)} %copy-done.73, bf16[1088,768]{1,0:T(8,128)(2,1)} %get-tuple-element.234, bf16[]{:T(256)} %constant.6847.clone.1), kind=kCustom, calls=%fused_computation.312 | custom fusion | bytes 395264 | tf_op jit(solution)/shard_map/scatter | solution.py:484
  188.3 8.1 %multiply_convert_fusion.8 = (bf16[4,256,1024]{2,1,0:T(8,128)(2,1)S(1)}, f32[4,256,1024]{2,1,0:T(8,128)}) fusion(f32[256,1024]{1,0:T(8,128)S(1)} %fusion.185, bf16[1024,1024]{1,0:T(8,128)(2,1)} %param.52, f32[4,256,1024]{2,1,0:T(8,128)} %fusion.82), kind=kOutput, calls=%fused_computation.88 | convolution fusion | flops 2159017984 | bytes 13631488 | tf_op jit(solution)/shard_map/rsw,wv->rsv/dot_general | solution.py:288
  203.2 8.9 %fusion.10 = f32[4,256,3072]{2,1,0:T(8,128)S(1)} fusion(bf16[4,256,1024]{2,1,0:T(8,128)(2,1)S(1)} %get-tuple-element.40, bf16[1024,3072]{1,0:T(8,128)(2,1)} %param.53), kind=kOutput, calls=%fused_computation.37 | convolution fusion | flops 6442450944 | bytes 20971520 | tf_op jit(solution)/shard_map/rsw,wv->rsv/dot_general | solution.py:291
  220.8 8.3 %fusion.166 = (f32[4,256]{1,0:T(4,128)S(1)}, f32[4,256,1024]{2,1,0:T(8,128)S(1)}, f32[4,256,1024]{2,1,0:T(8,128)}) fusion(f32[4,256,1024]{2,1,0:T(8,128)S(1)} %copy-done.2, f32[4,256,3072]{2,1,0:T(8,128)} %copy-done.3, bf16[1024,1024]{1,0:T(8,128)(2,1)S(1)} %copy-done.90, f32[4,256,1024]{2,1,0:T(8,128)S(1)} %fusion.46), kind=kOutput, calls=%fused_computation.451 | convolution fusion | flops 2155871232 | bytes 23072768 | tf_op jit(solution)/shard_map/rsw,wv->rsv/dot_general | solution.py:312
  262.0 8.1 %dynamic-slice_bitcast_fusion.2 = (bf16[2,2,2,2,32,4096]{5,4,3,2,1,0:T(8,128)(2,1)}, bf16[2,2,2,2,32,4096]{5,4,3,2,1,0:T(8,128)(2,1)}) fusion(bf16[2,2,2,2,2,32,4096]{6,5,4,3,2,1,0:T(8,128)(2,1)} %bitcast.560, s32[]{:T(128)S(6)} %select_n.806, s32[]{:T(128)S(6)} %select_n.805), kind=kLoop, calls=%fused_computation.73 | loop fusion | bytes 16777224 | tf_op jit(solution)/shard_map/jit(dynamic_index_in_dim)/squeeze | solution.py:197
  270.1 7.9 %fusion.164 = (f32[4,256]{1,0:T(4,128)}, f32[4,256]{1,0:T(4,128)}, bf16[4,256,1024]{2,1,0:T(8,128)(2,1)}, bf16[4,256,1024]{2,1,0:T(8,128)(2,1)}, f32[4,256,1024]{2,1,0:T(8,128)}) fusion(f32[4,256,3072]{2,1,0:T(8,128)} %copy-done.3, f32[4,256]{1,0:T(4,128)S(1)} %copy-done.70, f32[4,256,1024]{2,1,0:T(8,128)S(1)} %copy-done.2, f32[4,256]{1,0:T(4,128)S(1)} %copy-done.62, ...), kind=kOutput, calls=%fused_computation.449 | convolution fusion | flops 2157967360 | bytes 20987904 | tf_op jit(solution)/shard_map/rsv,wv->rsw/dot_general | solution.py:342
  283.9 8.0 %fusion.68 = bf16[1024,16]{0,1:T(8,128)(2,1)} fusion(f32[4,256,1024]{2,1,0:T(8,128)} %get-tuple-element.175, f32[4,256,1024]{2,1,0:T(8,128)} %copy-done.1, f32[4,256]{1,0:T(4,128)S(1)} %broadcast_multiply_fusion.6, f32[4,256]{1,0:T(4,128)S(1)} %broadcast_multiply_fusion.7, f32[4,256]{1,0:T(4,128)} %add_rsqrt_fusion.3, f32[4,256]{1,0:T(4,128)} %copy-done.61, ...), kind=kOutput, calls=%fused_computation.171 | convolution fusion | flops 44122112 | bytes 16916480 | tf_op jit(solution)/shard_map/rsw,rcs->wc/dot_general | solution.py:349
  305.8 10.1 %fusion.18 = f32[4,256,1024]{2,1,0:T(8,128)} fusion(bf16[1024,2048]{1,0:T(8,128)(2,1)} %param.56, bf16[4,256,1024]{2,1,0:T(8,128)(2,1)S(1)} %copy-done.43, bf16[4,256,1024]{2,1,0:T(8,128)(2,1)S(1)} %copy-done.45), kind=kOutput, calls=%fused_computation.66 | convolution fusion | flops 4303355904 | bytes 12582912 | tf_op jit(solution)/shard_map/rsv,wv->rsw/dot_general | solution.py:369
  324.5 12.6 %fusion.184 = (bf16[256,1024]{1,0:T(8,128)(2,1)}, bf16[4,256,1024]{2,1,0:T(8,128)(2,1)}) fusion(f32[4,256,1024]{2,1,0:T(8,128)} %get-tuple-element.286, f32[256,1024]{1,0:T(8,128)S(1)} %copy-done.54, f32[4,256,1024]{2,1,0:T(8,128)} %fusion.18, bf16[4,256,3072]{2,1,0:T(8,128)(2,1)S(1)} %pad_maximum_fusion.1, bf16[1024,3072]{1,0:T(8,128)(2,1)S(1)} %bitcast.591), kind=kOutput, calls=%fused_computation.468 | convolution fusion | flops 6454771712 | bytes 24641536 | tf_op jit(solution)/shard_map/rsv,wv->rsw/dot_general | solution.py:367
  381.2 10.1 %bitcast_convert_fusion = bf16[1024,3072]{1,0:T(8,128)(2,1)S(1)} fusion(bf16[4,256,1024]{2,1,0:T(8,128)(2,1)S(1)} %copy-done.102, bf16[4,256,3072]{2,1,0:T(8,128)(2,1)} %copy-done.34), kind=kOutput, calls=%fused_computation.24 | convolution fusion | flops 6445596672 | bytes 14680064 | tf_op jit(solution)/shard_map/rsw,rsv->wv/dot_general | solution.py:387
  391.3 10.5 %maximum_maximum_fusion = bf16[2,2,2,2,2,32,5120]{6,5,4,3,2,1,0:T(8,128)(2,1)} fusion(bf16[2,2,2,2,2,8,1024]{6,5,4,3,2,1,0:T(8,128)(2,1)S(1)} %bitcast.583, bf16[2,2,2,2,2,24,1024]{6,5,4,3,2,1,0:T(8,128)(2,1)S(1)} %bitcast.563, bf16[2,2,2,2,2,32,1024]{6,5,4,3,2,1,0:T(8,128)(2,1)S(1)} %bitcast.581, bf16[2,2,2,2,2,32,3072]{6,5,4,3,2,1,0:T(8,128)(2,1)S(1)} %bitcast.564), kind=kLoop, calls=%fused_computation.31 | loop fusion | flops 41943040 | bytes 20971520 | tf_op jit(solution)/shard_map/concatenate | solution.py:397
  413.3 9.1 %dynamic-slice_bitcast_fusion = (bf16[2,2,2,2,32,5120]{5,4,3,2,1,0:T(8,128)(2,1)}, bf16[2,2,2,2,32,5120]{5,4,3,2,1,0:T(8,128)(2,1)}) fusion(bf16[2,2,2,2,2,32,5120]{6,5,4,3,2,1,0:T(8,128)(2,1)} %maximum_maximum_fusion, s32[]{:T(128)S(6)} %select_n.806, s32[]{:T(128)S(6)} %select_n.805), kind=kLoop, calls=%fused_computation.39 | loop fusion | bytes 20971528 | tf_op jit(solution)/shard_map/jit(dynamic_index_in_dim)/squeeze | solution.py:197
  446.3 18.3 %add_convert_fusion = bf16[1088,3072]{1,0:T(8,128)(2,1)} fusion(f32[1088,3072]{1,0:T(8,128)} %get-tuple-element.179, bf16[1088,768]{1,0:T(8,128)(2,1)} %fusion.40, bf16[3072,768]{1,0:T(8,128)(2,1)} %param.47, f32[1088,3072]{1,0:T(8,128)} %get-tuple-element.284), kind=kOutput, calls=%fused_computation.9 | convolution fusion | flops 5180620800 | bytes 39813120 | tf_op jit(solution)/shard_map/dot_general | solution.py:41
  464.6 10.6 %convolution_convert_fusion.1 = bf16[3072,768]{1,0:T(8,128)(2,1)} fusion(bf16[1088,3072]{1,0:T(8,128)(2,1)} %copy-done.103, bf16[1088,768]{1,0:T(8,128)(2,1)} %fusion.40), kind=kOutput, calls=%fused_computation.42 | convolution fusion | flops 5136187392 | bytes 13074432 | tf_op jit(solution)/shard_map/dot_general | solution.py:35
  482.2 12.6 %multiply_reduce_fusion.4 = (bf16[768]{0:T(1024)(128)(2,1)}, f32[1088]{0:T(1024)S(1)}, f32[1088]{0:T(1024)}, bf16[768]{0:T(1024)(128)(2,1)}, f32[1088,768]{1,0:T(8,128)}) fusion(f32[1088,768]{1,0:T(8,128)S(1)} %copy-done.12, f32[1088]{0:T(1024)S(1)} %copy-done.71, f32[1088]{0:T(1024)S(1)} %copy-done.67, f32[768]{0:T(1024)S(1)} %copy-done.87, ...), kind=kOutput, calls=%fused_computation.115 | convolution fusion | flops 5141344256 | bytes 18111488 | tf_op jit(solution)/shard_map/dot_general | solution.py:41
  494.8 10.2 %convolution_convert_fusion.2 = bf16[768,3072]{1,0:T(8,128)(2,1)S(1)} fusion(bf16[1088,3072]{1,0:T(8,128)(2,1)} %add_convert_fusion, f32[1088,768]{1,0:T(8,128)S(1)} %copy-done.12, f32[768]{0:T(1024)S(1)} %copy-done.93, f32[768]{0:T(1024)S(1)} %copy-done.87, f32[1088]{0:T(1024)S(1)} %copy-done.71, f32[1088]{0:T(1024)S(1)} %copy-done.67), kind=kOutput, calls=%fused_computation.43 | convolution fusion | flops 5140365312 | bytes 14760448 | tf_op jit(solution)/shard_map/dot_general | solution.py:35
  549.1 9.7 %collective-permute-done.16 = bf16[32,5120]{1,0:T(8,128)(2,1)} collective-permute-done((bf16[32,5120]{1,0:T(8,128)(2,1)}, bf16[32,5120]{1,0:T(8,128)(2,1)}, u32[]{:S(2)}, u32[]{:S(2)}) %collective-permute-start.16) | collective-permute-done | bytes 327712 | tf_op jit(solution)/shard_map/ppermute | solution.py:162
  592.4 41.9 %attend_back.1 = (bf16[1088,768]{1,0:T(8,128)(2,1)}, bf16[1088,768]{1,0:T(8,128)(2,1)}, bf16[1088,768]{1,0:T(8,128)(2,1)}) custom-call(s32[1]{0:T(128)} %add_shard_map.6.len_ref, bf16[1088,2304]{1,0:T(8,128)(2,1)} %fusion.7.q_ref.k_ref.v_ref, bf16[1088,2304]{1,0:T(8,128)(2,1)} %fusion.7.q_ref.k_ref.v_ref, bf16[1088,2304]{1,0:T(8,128)(2,1)} %fusion.7.q_ref.k_ref.v_ref, ...), custom_call_target="tpu_custom_call" | custom-call | flops 9091153920 | bytes 15040512 | tf_op jit(solution)/shard_map/attend_back/pallas_call | solution.py:142
  671.9 8.2 %collective-permute-done.43 = bf16[24,6144]{1,0:T(8,128)(2,1)S(1)} collective-permute-done((bf16[24,6144]{1,0:T(8,128)(2,1)S(1)}, bf16[24,6144]{1,0:T(8,128)(2,1)S(1)}, u32[]{:S(2)}, u32[]{:S(2)}) %collective-permute-start.43) | collective-permute-done | bytes 294944 | tf_op jit(solution)/shard_map/ppermute | solution.py:162
  715.1 13.4 %collective-permute-done.34 = bf16[2,2,2,24,1536]{4,3,2,1,0:T(8,128)(2,1)S(1)} collective-permute-done((bf16[2,2,2,24,1536]{4,3,2,1,0:T(8,128)(2,1)S(1)}, bf16[2,2,2,24,1536]{4,3,2,1,0:T(8,128)(2,1)S(1)}, u32[]{:S(2)}, u32[]{:S(2)}) %collective-permute-start.34) | collective-permute-done | bytes 589856 | tf_op jit(solution)/shard_map/ppermute | solution.py:162
  (539 shorter events, 445.0 us)
Async XLA Ops:
  22.3 146.7 %all-to-all-start = ((bf16[8,2,256]{2,1,0:T(2,128)(2,1)}), bf16[8,2,256]{2,1,0:T(2,128)(2,1)}, u32[]{:S(2)}, u32[]{:S(2)}) async-start(bf16[8,2,256]{2,1,0:T(2,128)(2,1)} %reshape.1326), calls=%async_computation | async-start | bytes 16384 | tf_op jit(solution)/shard_map/all_to_all | solution.py:508
  169.0 17.2 %all-to-all-start.1 = ((bf16[8,32,768]{2,1,0:T(8,128)(2,1)}), bf16[8,32,768]{2,1,0:T(8,128)(2,1)}, u32[]{:S(2)}, u32[]{:S(2)}) async-start(bf16[8,32,768]{2,1,0:T(8,128)(2,1)} %bitcast.582), calls=%async_computation.1 | async-start | bytes 786432 | tf_op jit(solution)/shard_map/all_to_all | solution.py:501
  270.1 45.8 %collective-permute-start = (bf16[2,2,2,2,32,4096]{5,4,3,2,1,0:T(8,128)(2,1)}, bf16[2,2,2,2,32,4096]{5,4,3,2,1,0:T(8,128)(2,1)}, u32[]{:S(2)}, u32[]{:S(2)}) collective-permute-start(bf16[2,2,2,2,32,4096]{5,4,3,2,1,0:T(8,128)(2,1)} %get-tuple-element.189), channel_id=1, source_target_pairs={{0,1},{1,0},{2,3},{3,2},{4,5},{5,4},{6,7},{7,6},{8,9},{9,8},{10,11... | collective-permute-start | bytes 12582920 | tf_op jit(solution)/shard_map/ppermute | solution.py:162
  320.1 55.6 %collective-permute-start.1 = (bf16[2,2,2,32,2048]{4,3,2,1,0:T(8,128)(2,1)}, bf16[2,2,2,32,2048]{4,3,2,1,0:T(8,128)(2,1)}, u32[]{:S(2)}, u32[]{:S(2)}) collective-permute-start(bf16[2,2,2,32,2048]{4,3,2,1,0:T(8,128)(2,1)} %fusion.69), channel_id=1, source_target_pairs={{0,2},{1,3},{2,0},{3,1},{4,6},{5,7},{6,4},{7,5},{8,10},{9,11},{10,... | collective-permute-start | bytes 3145736 | tf_op jit(solution)/shard_map/ppermute | solution.py:162
  323.0 56.0 %collective-permute-start.3 = (bf16[2,2,2,32,2048]{4,3,2,1,0:T(8,128)(2,1)}, bf16[2,2,2,32,2048]{4,3,2,1,0:T(8,128)(2,1)}, u32[]{:S(2)}, u32[]{:S(2)}) collective-permute-start(bf16[2,2,2,32,2048]{4,3,2,1,0:T(8,128)(2,1)} %fusion.70), channel_id=1, source_target_pairs={{0,4},{4,0},{8,12},{12,8},{16,20},{20,16},{24,28},{28,24},{1,5},{5... | collective-permute-start | bytes 3145736 | tf_op jit(solution)/shard_map/ppermute | solution.py:162
  377.4 24.4 %collective-permute-start.2 = (bf16[2,2,32,2048]{3,2,1,0:T(8,128)(2,1)S(1)}, bf16[2,2,32,2048]{3,2,1,0:T(8,128)(2,1)S(1)}, u32[]{:S(2)}, u32[]{:S(2)}) collective-permute-start(bf16[2,2,32,2048]{3,2,1,0:T(8,128)(2,1)S(1)} %fusion.72), channel_id=1, source_target_pairs={{0,4},{4,0},{8,12},{12,8},{16,20},{20,16},{24,28},{28,24},{1,5},{5... | collective-permute-start | bytes 1572872 | tf_op jit(solution)/shard_map/ppermute | solution.py:162
  380.6 23.7 %collective-permute-start.4 = (bf16[2,2,32,2048]{3,2,1,0:T(8,128)(2,1)S(1)}, bf16[2,2,32,2048]{3,2,1,0:T(8,128)(2,1)S(1)}, u32[]{:S(2)}, u32[]{:S(2)}) collective-permute-start(bf16[2,2,32,2048]{3,2,1,0:T(8,128)(2,1)S(1)} %fusion.71), channel_id=1, source_target_pairs={{0,2},{1,3},{2,0},{3,1},{4,6},{5,7},{6,4},{7,5},{8,10},{9,11},{10,... | collective-permute-start | bytes 1572872 | tf_op jit(solution)/shard_map/ppermute | solution.py:162
  408.2 19.0 %collective-permute-start.7 = (bf16[32,4096]{1,0:T(8,128)(2,1)}, bf16[32,4096]{1,0:T(8,128)(2,1)}, u32[]{:S(2)}, u32[]{:S(2)}) collective-permute-start(bf16[32,4096]{1,0:T(8,128)(2,1)} %pad_maximum_fusion.27), channel_id=1, source_target_pairs={{0,8},{4,12},{8,0},{12,4},{16,24},{20,28},{24,16},{28,20},{1,9},{5... | collective-permute-start | bytes 786440 | tf_op jit(solution)/shard_map/ppermute | solution.py:162
  422.3 18.0 %collective-permute-start.5 = (bf16[2,2,2,2,32,5120]{5,4,3,2,1,0:T(8,128)(2,1)}, bf16[2,2,2,2,32,5120]{5,4,3,2,1,0:T(8,128)(2,1)S(1)}, u32[]{:S(2)}, u32[]{:S(2)}) collective-permute-start(bf16[2,2,2,2,32,5120]{5,4,3,2,1,0:T(8,128)(2,1)} %get-tuple-element.183), channel_id=1, source_target_pairs={{0,1},{1,0},{2,3},{3,2},{4,5},{5,4},{6,7},{7,6},{8,9},{9,8},{10,11... | collective-permute-start | bytes 15728648 | tf_op jit(solution)/shard_map/ppermute | solution.py:162
  442.9 38.1 %collective-permute-start.9 = (bf16[2,2,2,32,2560]{4,3,2,1,0:T(8,128)(2,1)}, bf16[2,2,2,32,2560]{4,3,2,1,0:T(8,128)(2,1)}, u32[]{:S(2)}, u32[]{:S(2)}) collective-permute-start(bf16[2,2,2,32,2560]{4,3,2,1,0:T(8,128)(2,1)} %fusion.54), channel_id=1, source_target_pairs={{0,2},{1,3},{2,0},{3,1},{4,6},{5,7},{6,4},{7,5},{8,10},{9,11},{10,... | collective-permute-start | bytes 3932168 | tf_op jit(solution)/shard_map/ppermute | solution.py:162
  445.6 35.3 %collective-permute-start.10 = (bf16[2,2,2,32,2560]{4,3,2,1,0:T(8,128)(2,1)}, bf16[2,2,2,32,2560]{4,3,2,1,0:T(8,128)(2,1)}, u32[]{:S(2)}, u32[]{:S(2)}) collective-permute-start(bf16[2,2,2,32,2560]{4,3,2,1,0:T(8,128)(2,1)} %fusion.55), channel_id=1, source_target_pairs={{0,4},{4,0},{8,12},{12,8},{16,20},{20,16},{24,28},{28,24},{1,5},{5... | collective-permute-start | bytes 3932168 | tf_op jit(solution)/shard_map/ppermute | solution.py:162
  528.4 30.4 %collective-permute-start.16 = (bf16[32,5120]{1,0:T(8,128)(2,1)}, bf16[32,5120]{1,0:T(8,128)(2,1)}, u32[]{:S(2)}, u32[]{:S(2)}) collective-permute-start(bf16[32,5120]{1,0:T(8,128)(2,1)} %pad_maximum_fusion.19), channel_id=1, source_target_pairs={{0,16},{4,20},{8,24},{12,28},{16,0},{20,4},{24,8},{28,12},{1,17},{... | collective-permute-start | bytes 983048 | tf_op jit(solution)/shard_map/ppermute | solution.py:162
  536.7 22.1 %collective-permute-start.17 = (bf16[32,5120]{1,0:T(8,128)(2,1)}, bf16[32,5120]{1,0:T(8,128)(2,1)}, u32[]{:S(2)}, u32[]{:S(2)}) collective-permute-start(bf16[32,5120]{1,0:T(8,128)(2,1)} %pad_maximum_fusion.20), channel_id=1, source_target_pairs={{0,8},{4,12},{8,0},{12,4},{16,24},{20,28},{24,16},{28,20},{1,9},{5... | collective-permute-start | bytes 983048 | tf_op jit(solution)/shard_map/ppermute | solution.py:162
  537.4 21.4 %collective-permute-start.18 = (bf16[32,5120]{1,0:T(8,128)(2,1)}, bf16[32,5120]{1,0:T(8,128)(2,1)}, u32[]{:S(2)}, u32[]{:S(2)}) collective-permute-start(bf16[32,5120]{1,0:T(8,128)(2,1)} %pad_maximum_fusion.21), channel_id=1, source_target_pairs={{0,24},{4,28},{8,16},{12,20},{16,8},{20,12},{24,0},{28,4},{1,25},{... | collective-permute-start | bytes 983048 | tf_op jit(solution)/shard_map/ppermute | solution.py:162
  548.4 35.0 %collective-permute-start.14 = (bf16[2,2,2,2,24,6144]{5,4,3,2,1,0:T(8,128)(2,1)}, bf16[2,2,2,2,24,6144]{5,4,3,2,1,0:T(8,128)(2,1)}, u32[]{:S(2)}, u32[]{:S(2)}) collective-permute-start(bf16[2,2,2,2,24,6144]{5,4,3,2,1,0:T(8,128)(2,1)} %get-tuple-element.185), channel_id=1, source_target_pairs={{0,1},{1,0},{2,3},{3,2},{4,5},{5,4},{6,7},{7,6},{8,9},{9,8},{10,11... | collective-permute-start | bytes 14155784 | tf_op jit(solution)/shard_map/ppermute | solution.py:162
  587.9 46.4 %collective-permute-start.19 = (bf16[2,2,2,24,3072]{4,3,2,1,0:T(8,128)(2,1)}, bf16[2,2,2,24,3072]{4,3,2,1,0:T(8,128)(2,1)}, u32[]{:S(2)}, u32[]{:S(2)}) collective-permute-start(bf16[2,2,2,24,3072]{4,3,2,1,0:T(8,128)(2,1)} %fusion.61), channel_id=1, source_target_pairs={{0,2},{1,3},{2,0},{3,1},{4,6},{5,7},{6,4},{7,5},{8,10},{9,11},{10,... | collective-permute-start | bytes 3538952 | tf_op jit(solution)/shard_map/ppermute | solution.py:162
  591.2 46.6 %collective-permute-start.20 = (bf16[2,2,2,24,3072]{4,3,2,1,0:T(8,128)(2,1)}, bf16[2,2,2,24,3072]{4,3,2,1,0:T(8,128)(2,1)}, u32[]{:S(2)}, u32[]{:S(2)}) collective-permute-start(bf16[2,2,2,24,3072]{4,3,2,1,0:T(8,128)(2,1)} %fusion.62), channel_id=1, source_target_pairs={{0,4},{4,0},{8,12},{12,8},{16,20},{20,16},{24,28},{28,24},{1,5},{5... | collective-permute-start | bytes 3538952 | tf_op jit(solution)/shard_map/ppermute | solution.py:162
  657.6 22.5 %collective-permute-start.43 = (bf16[24,6144]{1,0:T(8,128)(2,1)S(1)}, bf16[24,6144]{1,0:T(8,128)(2,1)S(1)}, u32[]{:S(2)}, u32[]{:S(2)}) collective-permute-start(bf16[24,6144]{1,0:T(8,128)(2,1)S(1)} %pad_maximum_fusion.23), channel_id=1, source_target_pairs={{0,16},{4,20},{8,24},{12,28},{16,0},{20,4},{24,8},{28,12},{1,17},{... | collective-permute-start | bytes 884744 | tf_op jit(solution)/shard_map/ppermute | solution.py:162
  664.0 20.6 %collective-permute-start.45 = (bf16[24,6144]{1,0:T(8,128)(2,1)S(1)}, bf16[24,6144]{1,0:T(8,128)(2,1)S(1)}, u32[]{:S(2)}, u32[]{:S(2)}) collective-permute-start(bf16[24,6144]{1,0:T(8,128)(2,1)S(1)} %pad_maximum_fusion.25), channel_id=1, source_target_pairs={{0,24},{4,28},{8,16},{12,20},{16,8},{20,12},{24,0},{28,4},{1,25},{... | collective-permute-start | bytes 884744 | tf_op jit(solution)/shard_map/ppermute | solution.py:162
  708.8 22.1 %collective-permute-start.24 = (bf16[8,5248]{1,0:T(8,128)(2,1)}, bf16[8,5248]{1,0:T(8,128)(2,1)S(1)}, u32[]{:S(2)}, u32[]{:S(2)}) collective-permute-start(bf16[8,5248]{1,0:T(8,128)(2,1)} %concatenate.171), channel_id=1, source_target_pairs={{0,3},{1,2},{2,1},{3,0},{4,7},{5,6},{6,5},{7,4},{8,11},{9,10},{10,... | collective-permute-start | bytes 251912 | tf_op jit(solution)/shard_map/ppermute | solution.py:162
  710.0 20.9 %collective-permute-start.23 = (bf16[8,5248]{1,0:T(8,128)(2,1)}, bf16[8,5248]{1,0:T(8,128)(2,1)S(1)}, u32[]{:S(2)}, u32[]{:S(2)}) collective-permute-start(bf16[8,5248]{1,0:T(8,128)(2,1)} %concatenate.171), channel_id=1, source_target_pairs={{0,2},{1,3},{2,0},{3,1},{4,6},{5,7},{6,4},{7,5},{8,10},{9,11},{10,... | collective-permute-start | bytes 251912 | tf_op jit(solution)/shard_map/ppermute | solution.py:162
  710.7 20.2 %collective-permute-start.22 = (bf16[8,5248]{1,0:T(8,128)(2,1)}, bf16[8,5248]{1,0:T(8,128)(2,1)S(1)}, u32[]{:S(2)}, u32[]{:S(2)}) collective-permute-start(bf16[8,5248]{1,0:T(8,128)(2,1)} %concatenate.171), channel_id=1, source_target_pairs={{0,1},{1,0},{2,3},{3,2},{4,5},{5,4},{6,7},{7,6},{8,9},{9,8},{10,11... | collective-permute-start | bytes 251912 | tf_op jit(solution)/shard_map/ppermute | solution.py:162
  731.4 18.2 %collective-permute-start.25 = (bf16[5248]{0:T(1024)(128)(2,1)S(1)}, bf16[5248]{0:T(1024)(128)(2,1)S(1)}, u32[]{:S(2)}, u32[]{:S(2)}) collective-permute-start(bf16[5248]{0:T(1024)(128)(2,1)S(1)} %get-tuple-element.163), channel_id=1, source_target_pairs={{0,4},{4,0},{8,12},{12,8},{16,20},{20,16},{24,28},{28,24},{1,5},{5... | collective-permute-start | bytes 31496 | tf_op jit(solution)/shard_map/ppermute | solution.py:162
  732.8 19.2 %collective-permute-start.31 = (bf16[5248]{0:T(1024)(128)(2,1)S(1)}, bf16[5248]{0:T(1024)(128)(2,1)S(1)}, u32[]{:S(2)}, u32[]{:S(2)}) collective-permute-start(bf16[5248]{0:T(1024)(128)(2,1)S(1)} %get-tuple-element.164), channel_id=1, source_target_pairs={{0,28},{4,24},{8,20},{12,16},{16,12},{20,8},{24,4},{28,0},{1,29},{... | collective-permute-start | bytes 31496 | tf_op jit(solution)/shard_map/ppermute | solution.py:162
  (137 other events, 1542.0 us)
